TPU v7x, 512 devices: a whole 4x8x8 slice. The times are simulated.
512 devices in a mesh: section: 4 (over x), seq: 128 (over z, y, core).
Axes of the slice: x: 4, y: 8, z: 8, core: 2. Of those that a mesh axis runs over, the one named last changes fastest.
Arguments:
- hidden: bfloat16 [65536, 4096], P('seq', 'section'), may hold values from -6 to 6
- norm_gain: bfloat16 [4096], P('section'), may hold values from 0.25 to 1.75
- query_weight: bfloat16 [4096, 512], P(None, 'section')
- key_weight: bfloat16 [4096, 128], P('section')
- value_weight: bfloat16 [4096, 128], P('section'), may hold values from -0.5 to 0.5
- output_weight: bfloat16 [512, 4096], P(None, 'section'), may hold values from -0.25 to 0.25
- block_reach: int32 [512], P('seq'), may hold values from 0 to 2
- header_ids: int32 [2], replicated, may hold values from 0 to 511, as said below
Outputs:
- attention_out: bfloat16 [65536, 4096], P('seq', 'section')
Inputs may be any that keep to these rules, and one draw needn't show every extreme that they name: `header_ids`: the 2 indices are distinct block indices, and the last block, 511, is always one of them, at any position.
All inputs are finite; a program needn't handle non-finite values.
Results may differ from a plain program's by a relative error of at most 0.014.
Values may be sent and summed in bfloat16 or wider, within the bound.
No kernel may reach another device: no remote copies, remote signals or barrier semaphores. Data moves between devices by JAX's collectives and lax.ppermute only.
A program may use at most 64 MiB of HBM per device.

v0:
```python
import math
import jax
import jax.numpy as jnp
from jax import lax
from jax.sharding import PartitionSpec as P

BLOCK = 128
REACH = 2
EPSILON = 1e-05
THETA = 500000.0


def merged(value, axis, combine):
    everything = jax.tree.map(lambda part: lax.all_gather(part, axis), value)
    leading = jax.tree.map(lambda part: part[0], everything)

    def lap(k, so_far):
        return combine(so_far, jax.tree.map(lambda part: part[k], everything))

    return lax.fori_loop(1, lax.axis_size(axis), lap, leading)


def padded(cells, sides, width):
    for axis, dim in sides:
        count = lax.axis_size(axis)
        ends = count - 1
        head = lax.slice_in_dim(cells, 0, width, axis=dim)
        tail = lax.slice_in_dim(cells, cells.shape[dim] - width, cells.shape[dim], axis=dim)
        cells = jnp.concatenate(
            [
                lax.ppermute(tail, axis, [(i, (i + 1) % count) for i in range(ends)]),
                cells,
                lax.ppermute(head, axis, [((i + 1) % count, i) for i in range(ends)]),
            ],
            axis=dim,
        )
    return cells


def tables(positions, head_width):
    middle = head_width // 2
    frequency = jnp.exp(
        -(2.0 / head_width) * math.log(THETA) * jnp.arange(middle, dtype=jnp.float32)
    )
    angles = positions.astype(jnp.float32)[:, None] * frequency[None, :]
    angles = jnp.concatenate([angles, angles], axis=1)
    return (jnp.cos(angles), jnp.sin(angles))


def rotate(values, cosine_table, sine_table):
    middle = values.shape[-1] // 2
    turned = jnp.concatenate([-values[..., middle:], values[..., :middle]], axis=-1)
    return values * cosine_table + turned * sine_table


def combine_parts(earlier, later):
    first_max, first_total, first_out = earlier
    second_max, second_total, second_out = later
    overall = jnp.maximum(first_max, second_max)
    first_factor = jnp.exp(first_max - overall)
    second_factor = jnp.exp(second_max - overall)
    return (
        overall,
        first_total * first_factor + second_total * second_factor,
        first_out * first_factor[:, None] + second_out * second_factor[:, None],
    )


def on_device(
    hidden,
    norm_gain,
    query_weight,
    key_weight,
    value_weight,
    output_weight,
    block_reach,
    header_ids,
):
    row_count = hidden.shape[0]
    part_width = hidden.shape[1]
    head_width = key_weight.shape[1]
    local_blocks = row_count // BLOCK
    total_blocks = local_blocks * lax.axis_size("seq")
    seq_place = lax.axis_index("seq")
    floats = hidden.astype(jnp.float32)
    squares = lax.psum(jnp.sum(floats * floats, axis=1), "section")
    scaling = lax.rsqrt(squares / (part_width * lax.axis_size("section")) + EPSILON)
    normed_part = (floats * scaling[:, None] * norm_gain.astype(jnp.float32)[None, :]).astype(
        jnp.bfloat16
    )
    weight_rows = query_weight
    query_sum = jnp.dot(
        lax.all_gather(normed_part, "section", axis=1, tiled=True),
        weight_rows,
        preferred_element_type=jnp.float32,
    )
    key_sum, value_sum = lax.psum(
        (
            jnp.dot(normed_part, key_weight, preferred_element_type=jnp.float32),
            jnp.dot(normed_part, value_weight, preferred_element_type=jnp.float32),
        ),
        "section",
    )
    positions = seq_place * row_count + jnp.arange(row_count, dtype=jnp.int32)
    cosine_table, sine_table = tables(positions, head_width)
    queries = rotate(query_sum, cosine_table, sine_table).astype(jnp.bfloat16)
    keys_here = rotate(key_sum, cosine_table, sine_table).astype(jnp.bfloat16)
    values_here = value_sum.astype(jnp.bfloat16)
    packed = jnp.concatenate([queries, keys_here, values_here], axis=1)
    block_numbers = seq_place * local_blocks + jnp.arange(local_blocks, dtype=jnp.int32)
    select = header_ids[:, None] == block_numbers[None, :]
    shaped = packed.reshape(local_blocks, BLOCK, 3 * head_width)
    picked = jnp.einsum(
        "hb,bre->hre", select.astype(jnp.bfloat16), shaped, preferred_element_type=jnp.float32
    )
    header_pack = lax.psum(picked, "seq").astype(jnp.bfloat16).reshape(-1, 3 * head_width)
    head_queries = header_pack[:, :head_width]
    head_keys = header_pack[:, head_width : 2 * head_width]
    head_values = header_pack[:, 2 * head_width :]
    inverse_root = 1.0 / math.sqrt(head_width)
    far_scores = (
        jnp.einsum("qd,kd->qk", head_queries, keys_here, preferred_element_type=jnp.float32)
        * inverse_root
    )
    far_max = jnp.max(far_scores, axis=1)
    far_weights = jnp.exp(far_scores - far_max[:, None])
    far_total = jnp.sum(far_weights, axis=1)
    far_out = jnp.dot(
        far_weights.astype(jnp.bfloat16), values_here, preferred_element_type=jnp.float32
    )
    merged_max, merged_total, merged_out = merged(
        (far_max, far_total, far_out), "seq", combine_parts
    )
    header_result = merged_out / merged_total[:, None]
    margin_rows = REACH * BLOCK
    stacked = jnp.concatenate([keys_here, values_here], axis=1)
    extended = padded(stacked, (("seq", 0),), margin_rows)
    near_keys = extended[:, :head_width]
    near_values = extended[:, head_width:]
    extent = row_count + 2 * margin_rows
    key_blocks = seq_place * local_blocks - REACH + jnp.arange(extent, dtype=jnp.int32) // BLOCK
    query_blocks = seq_place * local_blocks + jnp.arange(row_count, dtype=jnp.int32) // BLOCK
    limits = jnp.repeat(block_reach, BLOCK)
    key_header = jnp.any(header_ids[:, None] == key_blocks[None, :], axis=0)
    allowed = (key_blocks >= 0)[None, :] & (key_blocks < total_blocks)[None, :]
    allowed = allowed & (jnp.abs(key_blocks[None, :] - query_blocks[:, None]) <= limits[:, None])
    allowed = allowed & jnp.logical_not(key_header)[None, :]
    near_scores = (
        jnp.einsum("qd,kd->qk", queries, near_keys, preferred_element_type=jnp.float32)
        * inverse_root
    )
    near_scores = jnp.where(allowed, near_scores, -jnp.inf)
    head_scores = (
        jnp.einsum("qd,kd->qk", queries, head_keys, preferred_element_type=jnp.float32)
        * inverse_root
    )
    scores = jnp.concatenate([near_scores, head_scores], axis=1)
    row_top = jnp.max(scores, axis=1)
    weights = jnp.exp(scores - row_top[:, None])
    row_sums = jnp.sum(weights, axis=1)
    joined = jnp.concatenate([near_values, head_values], axis=0)
    mixed_out = (
        jnp.dot(weights.astype(jnp.bfloat16), joined, preferred_element_type=jnp.float32)
        / row_sums[:, None]
    )
    header_local = jnp.einsum(
        "hb,hre->bre", select.astype(jnp.float32), header_result.reshape(-1, BLOCK, head_width)
    )
    is_local_header = jnp.any(select, axis=0)
    attended = jnp.where(
        is_local_header[:, None, None],
        header_local,
        mixed_out.reshape(local_blocks, BLOCK, head_width),
    )
    attended = attended.reshape(row_count, head_width).astype(jnp.bfloat16)
    weight_rows = output_weight
    result = jnp.dot(
        lax.all_gather(attended, "section", axis=1, tiled=True),
        weight_rows,
        preferred_element_type=jnp.float32,
    )
    return result.astype(jnp.bfloat16)


def solution(mesh):
    return jax.shard_map(
        on_device,
        mesh=mesh,
        in_specs=(
            P("seq", "section"),
            P("section"),
            P(None, "section"),
            P("section", None),
            P("section", None),
            P(None, "section"),
            P("seq"),
            P(),
        ),
        out_specs=P("seq", "section"),
        check_vma=False,
    )
```

profile of v0, /device:TPU:64, one launch (start us, length us, event | category | flops | bytes accessed | tf_op | source)
XLA Modules:
  0.0 913.6 jit_solution(16988144689448362159)
XLA Ops:
  7.3 1.5 fusion.2
  8.8 10.5 %psum.28 = f32[512]{0:T(512)S(1)} all-reduce(f32[512]{0:T(512)S(1)} %fusion.2), channel_id=1, replica_groups=mesh['section'=4,'seq'=128] {'section'}, use_global_device_ids=true, to_apply=%region_2.0 | all-reduce | flops 512 | bytes 4096 | tf_op jit(solution)/shard_map/psum | solution.py:86
  19.3 1.6 fusion.4
  20.9 1.2 fusion.53
  23.0 1.7 fusion.54
  24.8 17.2 %all-reduce.5 = bf16[512,128]{0,1:T(8,128)(2,1)S(1)} all-reduce(f32[512,128]{0,1:T(8,128)S(1)} %fusion.54), channel_id=1, replica_groups=mesh['section'=4,'seq'=128] {'section'}, use_global_device_ids=true, to_apply=%region_4.0 | all-reduce | flops 65536 | bytes 393216 | tf_op jit(solution)/shard_map/psum | solution.py:97
  42.0 34.5 %all-reduce.4.cloned.1.call-done = f32[512,128]{0,1:T(8,128)} async-done(((f32[512,128]{0,1:T(8,128)}), f32[512,128]{0,1:T(8,128)}) %all-reduce.4.cloned.1.call-update) | async-done | bytes 262160 | tf_op jit(solution)/shard_map/psum | solution.py:97
  77.5 55.5 %all-gather.8.cloned.1.call-done = bf16[512,4096]{1,0:T(8,128)(2,1)} async-done(((bf16[512,1024]{1,0:T(8,128)(2,1)}), bf16[512,4096]{1,0:T(8,128)(2,1)}) %all-gather.8.cloned.1.call-update) | async-done | bytes 4194320 | tf_op jit(solution)/shard_map/all_gather | solution.py:93
  133.0 3.7 fusion.52
  138.7 461.0 %all-reduce.6 = bf16[2,128,384]{2,0,1:T(2,128)(2,1)S(1)} all-reduce(f32[2,128,384]{2,0,1:T(2,128)S(1)} %fusion.48), channel_id=1, replica_groups=mesh['section'=4,'seq'=128] {'seq'}, use_global_device_ids=true, to_apply=%region_5.0 | all-reduce | flops 98304 | bytes 589824 | tf_op jit(solution)/shard_map/psum | solution.py:116
  601.6 82.4 %all-gather.3 = f32[128,1,256]{2,1,0:T(1,128)S(1)} all-gather(f32[1,1,256]{2,1,0:T(1,128)S(1)} %bitcast.66), channel_id=2, replica_groups=mesh['section'=4,'seq'=128] {'seq'}, dimensions={0}, use_global_device_ids=true | all-gather | bytes 132096 | tf_op jit(solution)/shard_map/all_gather | solution.py:14
  684.3 47.1 %all-gather.4 = f32[128,1,256]{2,1,0:T(1,128)S(1)} all-gather(f32[1,1,256]{2,1,0:T(1,128)S(1)} %bitcast.67), channel_id=3, replica_groups=mesh['section'=4,'seq'=128] {'seq'}, dimensions={0}, use_global_device_ids=true | all-gather | bytes 132096 | tf_op jit(solution)/shard_map/all_gather | solution.py:14
  731.4 4.6 collective-permute-start.1
  736.0 1.9 collective-permute-start
  738.5 5.9 collective-permute-done
  748.1 144.2 %while.19 = (s32[]{:T(128)}, f32[256]{0:T(256)S(1)}, f32[256]{0:T(256)S(1)}, f32[256,128]{1,0:T(8,128)S(1)}, f32[128,256]{1,0:T(8,128)S(1)}, /*index=5*/f32[128,...) while((s32[]{:T(128)}, f32[256]{0:T(256)S(1)}, f32[256]{0:T(256)S(1)}, ...), condition=%wide.region_9.10_spmd, body=%wide.region_8.0_spmd.sunk | while | flops 99845 | bytes 407703 | solution.py:20
  749.3 1.1 fusion.69
  751.5 1.1 fusion.69
  753.8 1.1 fusion.69
  754.9 1.1 fusion.69
  756.1 1.1 fusion.69
  757.2 1.1 fusion.69
  758.3 1.1 fusion.69
  759.5 1.1 fusion.69
  761.7 1.1 fusion.69
  764.0 1.1 fusion.69
  766.3 1.1 fusion.69
  768.6 1.1 fusion.69
  770.8 1.1 fusion.69
  773.1 1.1 fusion.69
  892.8 12.6 %all_gather.31 = bf16[512,512]{1,0:T(8,128)(2,1)S(1)} all-gather(bf16[512,128]{1,0:T(8,128)(2,1)S(1)} %bitcast.59), channel_id=1, replica_groups=mesh['section'=4,'seq'=128] {'section'}, dimensions={1}, use_global_device_ids=true | all-gather | bytes 655360 | tf_op jit(solution)/shard_map/all_gather | solution.py:178
  905.4 1.7 convolution_convert_fusion
  (442 shorter events, 136.4 us)
Async XLA Ops:
  6.5 898.9 %copy-start = (bf16[512,1024]{1,0:T(8,128)(2,1)S(1)}, bf16[512,1024]{1,0:T(8,128)(2,1)}, u32[]{:S(2)}) copy-start(bf16[512,1024]{1,0:T(8,128)(2,1)} %param.15) | copy-start | bytes 3145732
  6.5 14.4 %copy-start.7 = (bf16[1024,128]{1,0:T(8,128)(2,1)S(1)}, bf16[1024,128]{1,0:T(8,128)(2,1)}, u32[]{:S(2)}) copy-start(bf16[1024,128]{1,0:T(8,128)(2,1)} %param.13) | copy-start | bytes 786436
  6.5 70.0 %all-reduce.4.cloned.1.call-start = ((), (), s32[]{:S(2)}) async-start(), calls=%async_computation.1 | async-start | bytes 524288 | tf_op jit(solution)/shard_map/psum | solution.py:97
  19.3 3.6 copy-start.8
  20.9 1.3 copy-start.1
  22.1 110.9 %copy-start.4 = (bf16[4096,128]{1,0:T(8,128)(2,1)S(1)}, bf16[4096,128]{1,0:T(8,128)(2,1)}, u32[]{:S(2)}) copy-start(bf16[4096,128]{1,0:T(8,128)(2,1)} %param.12) | copy-start | bytes 3145732
  22.2 110.8 %all-gather.8.cloned.1.call-start = ((), (), s32[]{:S(2)}) async-start(), calls=%async_computation | async-start | bytes 5242880 | tf_op jit(solution)/shard_map/all_gather | solution.py:93
  22.9 724.2 %all-gather.10.cloned.1.call-start = ((), (), s32[]{:S(2)}) async-start(), calls=%async_computation.2 | async-start | bytes 16908288 | tf_op jit(solution)/shard_map/all_gather | solution.py:14
  77.5 59.2 %copy-start.3 = (f32[512,128]{0,1:T(8,128)S(1)}, f32[512,128]{0,1:T(8,128)}, u32[]{:S(2)}) copy-start(f32[512,128]{0,1:T(8,128)} %all-reduce.4.cloned.1.call-done) | copy-start | bytes 786436
  136.7 1.6 copy-start.9
  138.3 463.3 %copy-start.10 = (s32[4]{0:T(128)S(1)}, s32[4]{0:T(128)}, u32[]{:S(2)}) copy-start(s32[4]{0:T(128)} %param.16) | copy-start | bytes 52
  684.1 61.5 %copy-start.6 = (f32[128,1,256]{2,1,0:T(1,128)}, f32[128,1,256]{2,1,0:T(1,128)S(1)}, u32[]{:S(2)}) copy-start(f32[128,1,256]{2,1,0:T(1,128)S(1)} %all-gather.3) | copy-start | bytes 393220
  731.4 14.1 %copy-start.5 = (f32[128,1,256]{2,1,0:T(1,128)}, f32[128,1,256]{2,1,0:T(1,128)S(1)}, u32[]{:S(2)}) copy-start(f32[128,1,256]{2,1,0:T(1,128)S(1)} %all-gather.4) | copy-start | bytes 393220
  731.4 7.1 collective-permute-start.1
  736.0 8.4 collective-permute-start
  744.5 1.1 copy-start.2
  745.6 1.0 slice-start
  746.5 1.5 slice-start.1
  746.5 1.5 slice-start.2
Sparse Core Ops, SparseCore 0:
  22.3 54.2 all-reduce.3
  78.9 54.1 all-gather.7
  601.4 126.7 all-gather.9
where the time goes:
time: 916 us; the launch traced here: 914 us
  blocking collectives  631 us (69%)
  other arithmetic  146 us (16%)
  waiting for transfers between devices  96.8 us (11%)
  between operations  13.5 us (1%)
  matrix products  12.3 us (1%)
    psum x1, blocking collectives, on_device(): lax.psum(picked, 'seq').astype(jnp.bfloat16).reshape(-1, 3 * head_width)  461 us
    add x127, other arithmetic, combine_parts(): first_out * first_factor[:, None] + second_out * second_factor[:, None]  136 us
    all_gather x2, blocking collectives, merged(): everything = jax.tree.map(lambda part: lax.all_gather(part, axis), value)  130 us
    all_gather x1, waiting for transfers between devices, on_device(): lax.all_gather(normed_part, 'section', axis=1, tiled=True)  55.5 us
    psum x1, waiting for transfers between devices, on_device(): lax.psum((jnp.dot(normed_part, key_weight, preferred_element_type=jnp.flo...  34.5 us
  transfers between devices with their start and end apart: 5, of which 4 were waited for; matrix products, arithmetic and copies ran while one was open for 1% of the time, Pallas kernels for 0%

commit v1 on v0

--- a/solution.py
+++ b/solution.py
@@ -8,6 +8,11 @@
 REACH = 2
 EPSILON = 1e-05
 THETA = 500000.0
+
+
+def all_by_exchange(x, mesh_axis, d):
+    repeated = jnp.stack([x] * lax.axis_size(mesh_axis))
+    return jnp.concatenate(lax.all_to_all(repeated, mesh_axis, 0, 0), axis=d)
 
 
 def merged(value, axis, combine):
@@ -90,9 +95,7 @@
     )
     weight_rows = query_weight
     query_sum = jnp.dot(
-        lax.all_gather(normed_part, "section", axis=1, tiled=True),
-        weight_rows,
-        preferred_element_type=jnp.float32,
+        all_by_exchange(normed_part, "section", 1), weight_rows, preferred_element_type=jnp.float32
     )
     key_sum, value_sum = lax.psum(
         (

time: 916 us -> 887 us (0.968)
  waiting for transfers between devices: 96.8 us -> 20.9 us
  blocking collectives: 631 us -> 671 us
    all_gather x1 -> x0, waiting for transfers between devices: 55.5 us -> none  [on_device(): lax.all_gather(normed_part, 'section', axis=1, tiled=True)]
    psum x1, blocking collectives: 17.2 us -> 59.8 us  [on_device(): lax.psum((jnp.dot(normed_part, key_weight, preferred_element_type=jnp.flo...]
    psum x1, waiting for transfers between devices: 34.5 us -> 14.8 us  [on_device(): lax.psum((jnp.dot(normed_part, key_weight, preferred_element_type=jnp.flo...]
  transfers between devices with their start and end apart: 5 -> 5, of which waited for: 4 -> 3; matrix products, arithmetic and copies ran while one was open for 1% -> 1% of each run, Pallas kernels for 0% -> 0%
where the time goes in v1:
time: 887 us; the launch traced here: 885 us
  blocking collectives  671 us (76%)
  other arithmetic  146 us (16%)
  waiting for transfers between devices  20.9 us (2%)
  between operations  13.8 us (2%)
  starting transfers between devices  11.5 us (1%)
  matrix products  10.7 us (1%)
    psum x1, blocking collectives, on_device(): lax.psum(picked, 'seq').astype(jnp.bfloat16).reshape(-1, 3 * head_width)  459 us
    add x127, other arithmetic, combine_parts(): first_out * first_factor[:, None] + second_out * second_factor[:, None]  136 us
    all_gather x2, blocking collectives, merged(): everything = jax.tree.map(lambda part: lax.all_gather(part, axis), value)  130 us
    psum x1, blocking collectives, on_device(): lax.psum((jnp.dot(normed_part, key_weight, preferred_element_type=jnp.flo...  59.8 us
  transfers between devices with their start and end apart: 5, of which 3 were waited for; matrix products, arithmetic and copies ran while one was open for 1% of the time, Pallas kernels for 0%

profile of v1, /device:TPU:64, one launch (start us, length us, event | category | flops | bytes accessed | tf_op | source)
XLA Modules:
  0.0 884.7 jit_solution(12834288926780357710)
XLA Ops:
  7.3 1.5 fusion.2
  8.8 10.5 %psum.28 = f32[512]{0:T(512)S(1)} all-reduce(f32[512]{0:T(512)S(1)} %fusion.2), channel_id=1, replica_groups=mesh['section'=4,'seq'=128] {'section'}, use_global_device_ids=true, to_apply=%region_2.0 | all-reduce | flops 512 | bytes 4096 | tf_op jit(solution)/shard_map/psum | solution.py:91
  19.3 1.5 fusion.4
  21.4 2.3 stack.2
  23.7 5.0 all-to-all-start
  28.8 1.2 fusion.53
  30.7 59.8 %all-reduce.5 = bf16[512,128]{0,1:T(8,128)(2,1)S(1)} all-reduce(f32[512,128]{0,1:T(8,128)S(1)} %fusion.54), channel_id=1, replica_groups=mesh['section'=4,'seq'=128] {'section'}, use_global_device_ids=true, to_apply=%region_4.0 | all-reduce | flops 65536 | bytes 393216 | tf_op jit(solution)/shard_map/psum | solution.py:100
  90.5 14.8 %all-reduce.4.cloned.1.call-done = f32[512,128]{0,1:T(8,128)} async-done(((f32[512,128]{0,1:T(8,128)}), f32[512,128]{0,1:T(8,128)}) %all-reduce.4.cloned.1.call-update) | async-done | bytes 262160 | tf_op jit(solution)/shard_map/psum | solution.py:100
  106.3 3.3 fusion.52
  111.6 458.9 %all-reduce.6 = bf16[2,128,384]{2,0,1:T(2,128)(2,1)S(1)} all-reduce(f32[2,128,384]{2,0,1:T(2,128)S(1)} %fusion.48), channel_id=1, replica_groups=mesh['section'=4,'seq'=128] {'seq'}, use_global_device_ids=true, to_apply=%region_5.0 | all-reduce | flops 98304 | bytes 589824 | tf_op jit(solution)/shard_map/psum | solution.py:119
  572.4 82.4 %all-gather.3 = f32[128,1,256]{2,1,0:T(1,128)S(1)} all-gather(f32[1,1,256]{2,1,0:T(1,128)S(1)} %bitcast.69), channel_id=2, replica_groups=mesh['section'=4,'seq'=128] {'seq'}, dimensions={0}, use_global_device_ids=true | all-gather | bytes 132096 | tf_op jit(solution)/shard_map/all_gather | solution.py:19
  655.1 47.1 %all-gather.4 = f32[128,1,256]{2,1,0:T(1,128)S(1)} all-gather(f32[1,1,256]{2,1,0:T(1,128)S(1)} %bitcast.70), channel_id=3, replica_groups=mesh['section'=4,'seq'=128] {'seq'}, dimensions={0}, use_global_device_ids=true | all-gather | bytes 132096 | tf_op jit(solution)/shard_map/all_gather | solution.py:19
  702.2 4.5 collective-permute-start.1
  706.8 1.9 collective-permute-start
  709.3 5.9 collective-permute-done
  718.8 144.2 %while.19 = (s32[]{:T(128)}, f32[256]{0:T(256)S(1)}, f32[256]{0:T(256)S(1)}, f32[256,128]{1,0:T(8,128)S(1)}, f32[128,256]{1,0:T(8,128)S(1)}, /*index=5*/f32[128,...) while((s32[]{:T(128)}, f32[256]{0:T(256)S(1)}, f32[256]{0:T(256)S(1)}, ...), condition=%wide.region_9.10_spmd, body=%wide.region_8.0_spmd.sunk | while | flops 99845 | bytes 407703 | solution.py:25
  720.0 1.1 fusion.69
  721.1 1.1 fusion.69
  722.3 1.1 fusion.69
  723.4 1.1 fusion.69
  724.5 1.1 fusion.69
  725.7 1.1 fusion.69
  727.9 1.1 fusion.69
  730.2 1.1 fusion.69
  732.5 1.1 fusion.69
  734.8 1.1 fusion.69
  737.0 1.1 fusion.69
  739.3 1.1 fusion.69
  741.6 1.1 fusion.69
  742.7 1.1 fusion.69
  863.5 12.7 %all_gather.27 = bf16[512,512]{1,0:T(8,128)(2,1)S(1)} all-gather(bf16[512,128]{1,0:T(8,128)(2,1)S(1)} %bitcast.62), channel_id=1, replica_groups=mesh['section'=4,'seq'=128] {'section'}, dimensions={1}, use_global_device_ids=true | all-gather | bytes 655360 | tf_op jit(solution)/shard_map/all_gather | solution.py:181
  876.2 1.7 convolution_convert_fusion
  (439 shorter events, 136.7 us)
Async XLA Ops:
  6.5 869.7 %copy-start = (bf16[512,1024]{1,0:T(8,128)(2,1)S(1)}, bf16[512,1024]{1,0:T(8,128)(2,1)}, u32[]{:S(2)}) copy-start(bf16[512,1024]{1,0:T(8,128)(2,1)} %param.15) | copy-start | bytes 3145732
  23.7 5.1 copy-start.5
  23.7 6.3 copy-start.6
  23.7 82.5 %all-to-all-start = ((bf16[4,512,1024]{1,2,0:T(8,128)(2,1)}), bf16[4,512,1024]{1,2,0:T(8,128)(2,1)}, u32[]{:S(2)}, u32[]{:S(2)}) async-start(bf16[4,512,1024]{1,2,0:T(8,128)(2,1)} %stack.2), calls=%async_computation | async-start | bytes 8388608 | tf_op jit(solution)/shard_map/all_to_all | solution.py:15
  28.7 76.5 %all-reduce.4.cloned.1.call-start = ((), (), s32[]{:S(2)}) async-start(), calls=%async_computation.1 | async-start | bytes 524288 | tf_op jit(solution)/shard_map/psum | solution.py:100
  30.0 687.9 %all-gather.7.cloned.1.call-start = ((), (), s32[]{:S(2)}) async-start(), calls=%async_computation.2 | async-start | bytes 16908288 | tf_op jit(solution)/shard_map/all_gather | solution.py:19
  106.2 3.4 copy-start.2
  109.6 1.6 copy-start.7
  111.2 461.2 %copy-start.8 = (s32[4]{0:T(128)S(1)}, s32[4]{0:T(128)}, u32[]{:S(2)}) copy-start(s32[4]{0:T(128)} %param.16) | copy-start | bytes 52
  654.8 61.4 %copy-start.4 = (f32[128,1,256]{2,1,0:T(1,128)}, f32[128,1,256]{2,1,0:T(1,128)S(1)}, u32[]{:S(2)}) copy-start(f32[128,1,256]{2,1,0:T(1,128)S(1)} %all-gather.3) | copy-start | bytes 393220
  702.2 14.1 %copy-start.3 = (f32[128,1,256]{2,1,0:T(1,128)}, f32[128,1,256]{2,1,0:T(1,128)S(1)}, u32[]{:S(2)}) copy-start(f32[128,1,256]{2,1,0:T(1,128)S(1)} %all-gather.4) | copy-start | bytes 393220
  702.2 7.0 collective-permute-start.1
  706.8 8.4 collective-permute-start
  715.2 1.1 copy-start.1
  716.3 1.0 slice-start
  717.2 1.5 slice-start.1
  717.2 1.5 slice-start.2
Sparse Core Ops, SparseCore 0:
  31.9 73.3 all-reduce.3
  572.2 127.0 all-gather.6
